TPU v7x, 32 devices: a whole 2x2x4 slice. The times are simulated.
32 devices in a mesh: groups: 2 (over x), dev: 8 (over z, y), tp: 2 (over core).
Axes of the slice: x: 2, y: 2, z: 4, core: 2. Of those that a mesh axis runs over, the one named last changes fastest.
Arguments:
- h_in: bfloat16 [256, 4096], P(('groups', 'dev')), parts along dimension 0, may hold values from -6 to 6
- query: bfloat16 [256, 8192], P(('groups', 'dev'), 'tp'), parts along dimension 0, may hold values from -200 to 200
- key_cache: bfloat16 [256, 128, 512], P(('groups', 'dev'), None, 'tp'), parts along dimension 0, may hold values from -8 to 8
- cached_value_rows: bfloat16 [256, 128, 512], P(('groups', 'dev'), None, 'tp'), parts along dimension 0, may hold values from -6 to 6
- fresh_token_key: bfloat16 [256, 512], P(('groups', 'dev'), 'tp'), parts along dimension 0, may hold values from -6 to 6
- fresh_token_value: bfloat16 [256, 512], P(('groups', 'dev'), 'tp'), parts along dimension 0, may hold values from -6 to 6
- lengths: int32 [256], P(('groups', 'dev')), parts along dimension 0, may hold values from 2 to 128, as said below
- routes: int32 [256, 2], P(('groups', 'dev')), parts along dimension 0, may hold values from 0 to 3, all different within a row; in each aligned block of 16 rows (0 to 15, 16 to 31, ...) at most 12 rows name the same one
- w_out: bfloat16 [8192, 4096], P('tp', 'dev'), may hold values from -0.0625 to 0.0625
- gain: bfloat16 [4096], replicated, may hold values from 0.099609375 to 1.8984375
- router_weight: bfloat16 [4096, 4], replicated, may hold values from -0.09375 to 0.09375
- w_gate: bfloat16 [8, 4096, 768], P('dev', None, 'tp'), may hold values from -0.09375 to 0.09375
- w_up: bfloat16 [8, 4096, 768], P('dev', None, 'tp'), may hold values from -0.09375 to 0.09375
- w_down: bfloat16 [8, 768, 4096], P('dev', 'tp'), may hold values from -0.15625 to 0.15625
Outputs:
- mixed: bfloat16 [256, 4096], P(('groups', 'dev'), 'tp'), parts along dimension 0
There are 2 independent parts, one for each index of `groups`. A program takes and returns all parts, laid end to end along the dimension named above; an argument that names none is the same for every part. Nothing has to cross between parts.
Inputs may be any that keep to these rules, and one draw needn't show every extreme that they name: `routes`: within the 16 rows of one dev index no expert is named more than 12 times, a bound that some block reaches; each row names 2 different experts. `lengths`: some row uses all 128 slots.
All inputs are finite; a program needn't handle non-finite values.
Results may differ from a plain program's by a relative error of at most 0.0055.
Values may be sent and summed in bfloat16 or wider, within the bound.
A program may use at most 128 MiB of HBM per device.

v0:
```python
import math

import jax
import jax.numpy as jnp
from jax import lax
from jax.sharding import PartitionSpec as P

D = 4096
HEAD_SIZE = 128


epsilon = 1e-06


def attend(query, key_cache, cached_value_rows, fresh_token_key, fresh_token_value, lengths):
    count = query.shape[0]
    slots = key_cache.shape[1]
    kv_heads = key_cache.shape[2] // HEAD_SIZE
    queries = query.reshape(count, kv_heads, -1, HEAD_SIZE)
    keys_old = key_cache.reshape(count, slots, kv_heads, HEAD_SIZE)
    values_old = cached_value_rows.reshape(count, slots, kv_heads, HEAD_SIZE)
    keys_new = fresh_token_key.reshape(count, kv_heads, HEAD_SIZE)
    values_new = fresh_token_value.reshape(count, kv_heads, HEAD_SIZE)
    factor = 1.0 / math.sqrt(HEAD_SIZE)
    scores = (
        jnp.einsum("rgqd,rcgd->rgqc", queries, keys_old, preferred_element_type=jnp.float32)
        * factor
    )
    score_new = (
        jnp.einsum("rgqd,rgd->rgq", queries, keys_new, preferred_element_type=jnp.float32) * factor
    )
    positions = jnp.arange(slots, dtype=jnp.int32)
    live = (positions[None, :] < lengths[:, None])[:, None, None, :]
    scores = jnp.where(live, scores, -1e30)
    highest = jnp.maximum(jnp.max(scores, -1), score_new)
    expo = jnp.where(live, jnp.exp(scores - highest[..., None]), 0.0)
    expo_new = jnp.exp(score_new - highest)
    total = jnp.sum(expo, -1) + expo_new
    weights = (expo / total[..., None]).astype(jnp.bfloat16)
    weight_new = (expo_new / total).astype(jnp.bfloat16)
    blended = jnp.einsum("rgqc,rcgd->rgqd", weights, values_old, preferred_element_type=jnp.float32)
    blended = (
        blended
        + weight_new.astype(jnp.float32)[..., None] * values_new.astype(jnp.float32)[:, :, None, :]
    )
    return blended.astype(jnp.bfloat16).reshape(count, -1)


def expert_block(received, w_gate, w_up, w_down):
    flat_rows = received.reshape(-1, received.shape[2])
    gated = jnp.dot(flat_rows, w_gate[0], preferred_element_type=jnp.float32)
    upper = jnp.dot(flat_rows, w_up[0], preferred_element_type=jnp.float32)
    act = (jax.nn.silu(gated) * upper).astype(jnp.bfloat16)
    result = jnp.dot(act, w_down[0], preferred_element_type=jnp.float32)
    return result.reshape(received.shape[0], received.shape[1], -1)


def shards(
    h_in,
    query,
    key_cache,
    cached_value_rows,
    fresh_token_key,
    fresh_token_value,
    lengths,
    routes,
    w_out,
    gain,
    router_weight,
    w_gate,
    w_up,
    w_down,
):
    rows_here = query.shape[0]
    topk = routes.shape[1]
    experts = router_weight.shape[1]
    capacity = max(2, 3 * rows_here * topk // (2 * experts))
    tp_count = lax.axis_size("tp")
    tp_place = lax.axis_index("tp")
    half_width = D // tp_count
    attn = attend(query, key_cache, cached_value_rows, fresh_token_key, fresh_token_value, lengths)
    projected = jnp.dot(
        lax.all_gather(attn, "dev", axis=0, tiled=True), w_out, preferred_element_type=jnp.float32
    )
    partial_home = lax.all_to_all(projected, "dev", split_axis=0, concat_axis=1, tiled=True)
    residual = h_in.astype(jnp.float32)
    h_one = lax.psum(partial_home, "tp") + residual
    scale_rows = lax.rsqrt(jnp.mean(h_one * h_one, 1) + epsilon)
    normed = (h_one * scale_rows[:, None] * gain.astype(jnp.float32)[None, :]).astype(jnp.bfloat16)
    logits = jnp.dot(normed, router_weight, preferred_element_type=jnp.float32)
    h_half = lax.dynamic_slice_in_dim(h_one, tp_place * half_width, half_width, 1)
    expert_ids = jnp.arange(experts, dtype=jnp.int32)
    chosen = routes[:, :, None] == expert_ids[None, None, :]
    picked = jnp.sum(jnp.where(chosen, logits[:, None, :], 0.0), -1)
    expo = jnp.exp(picked)
    gates = expo / jnp.sum(expo, 1, keepdims=True)
    flat_routes = routes.reshape(-1)
    hits = (flat_routes[:, None] == expert_ids[None, :]).astype(jnp.int32)
    before = jnp.cumsum(hits, 0) - hits
    ranks = jnp.sum(before * hits, 1)
    slot_ids = (flat_routes * capacity + ranks).reshape(rows_here, topk)
    slot_range = jnp.arange(experts * capacity, dtype=jnp.int32)
    matches = slot_ids[:, :, None] == slot_range[None, None, :]
    selector = jnp.any(matches, 1).astype(jnp.bfloat16)
    combine_weights = jnp.sum(jnp.where(matches, gates[:, :, None], 0.0), 1)
    packed = jnp.einsum("rj,rw->jw", selector, normed, preferred_element_type=jnp.float32).astype(
        jnp.bfloat16
    )
    outgoing = jnp.concatenate([packed, packed], 0).reshape(2 * experts, capacity, -1)
    result = expert_block(
        lax.all_to_all(outgoing, "dev", split_axis=0, concat_axis=0, tiled=True),
        w_gate,
        w_up,
        w_down,
    )
    returned = lax.all_to_all(result, "dev", split_axis=0, concat_axis=0, tiled=True)
    per_slot = jnp.sum(returned.reshape(2, experts * capacity, -1), 0)
    moe = jnp.dot(
        combine_weights,
        per_slot,
        precision=lax.Precision.HIGHEST,
        preferred_element_type=jnp.float32,
    )
    moe = lax.psum_scatter(moe, "tp", scatter_dimension=1, tiled=True)
    return (h_half + moe).astype(jnp.bfloat16)


def solution(mesh):
    placed = (
        P(("groups", "dev"), None),
        P(("groups", "dev"), "tp"),
        P(("groups", "dev"), None, "tp"),
        P(("groups", "dev"), None, "tp"),
        P(("groups", "dev"), "tp"),
        P(("groups", "dev"), "tp"),
        P(("groups", "dev")),
        P(("groups", "dev"), None),
        P("tp", "dev"),
        P(),
        P(),
        P("dev", None, "tp"),
        P("dev", None, "tp"),
        P("dev", "tp", None),
    )
    return jax.shard_map(
        shards, mesh=mesh, in_specs=placed, out_specs=P(("groups", "dev"), "tp"), check_vma=False
    )
```

profile of v0, /device:TPU:0, one launch (start us, length us, event | category | flops | bytes accessed | tf_op | source)
XLA Modules:
  0.0 212.5 jit_solution(7106186256231484543)
XLA Ops:
  6.5 1.1 copy.48
  9.9 2.0 fusion.29
  12.3 1.7 fusion.7
  14.7 43.1 %all-gather.2.cloned.1.call-done = bf16[128,4096]{1,0:T(8,128)(2,1)} async-done(((bf16[16,4096]{1,0:T(8,128)(2,1)}), bf16[128,4096]{1,0:T(8,128)(2,1)}) %all-gather.2.cloned.1.call-update) | async-done | bytes 1048592 | tf_op jit(solution)/shard_map/all_gather | solution.py:83
  57.8 4.0 %fusion.31 = f32[128,512]{1,0:T(8,128)} fusion(bf16[128,4096]{1,0:T(8,128)(2,1)} %all-gather.2.cloned.1.call-done, bf16[4096,512]{1,0:T(8,128)(2,1)} %param.22), kind=kOutput, calls=%fused_computation.52 | convolution fusion | flops 536870912 | bytes 5505024 | tf_op jit(solution)/shard_map/dot_general | solution.py:82
  61.7 3.4 %all-to-all-start = ((f32[8,16,512]{2,1,0:T(8,128)}), f32[8,16,512]{2,1,0:T(8,128)S(1)}, u32[]{:S(2)}, u32[]{:S(2)}) async-start(f32[8,16,512]{2,1,0:T(8,128)} %bitcast.58), calls=%async_computation | async-start | bytes 524288 | tf_op jit(solution)/shard_map/all_to_all | solution.py:85
  65.9 7.5 %all-to-all-done = f32[8,16,512]{2,1,0:T(8,128)S(1)} async-done(((f32[8,16,512]{2,1,0:T(8,128)}), f32[8,16,512]{2,1,0:T(8,128)S(1)}, u32[]{:S(2)}, u32[]{:S(2)}) %all-to-all-start) | async-done | bytes 262176 | tf_op jit(solution)/shard_map/all_to_all | solution.py:85
  74.3 17.1 %all-reduce.2.cloned.1.call-done = f32[16,4096]{1,0:T(8,128)} async-done(((f32[16,4096]{1,0:T(8,128)}), f32[16,4096]{1,0:T(8,128)}) %all-reduce.2.cloned.1.call-update) | async-done | bytes 262160 | tf_op jit(solution)/shard_map/psum | solution.py:87
  91.4 1.1 multiply_reduce_fusion
  92.9 1.0 pad_maximum_fusion
  93.9 2.2 %reshape.97 = bf16[8,12,4096]{2,1,0:T(8,128)(2,1)} reshape(bf16[96,4096]{1,0:T(8,128)(2,1)} %pad_maximum_fusion) | data formatting | bytes 1572864 | tf_op jit(solution)/shard_map/reshape | solution.py:109
  96.0 32.1 %all_to_all.29 = bf16[8,12,4096]{2,1,0:T(8,128)(2,1)} all-to-all(bf16[8,12,4096]{2,1,0:T(8,128)(2,1)} %reshape.97), channel_id=1, replica_groups=mesh['groups'=2,'dev'=8,'tp'=2] {'dev'}, dimensions={0} | all-to-all | bytes 1572864 | tf_op jit(solution)/shard_map/all_to_all | solution.py:111
  128.1 2.2 %reshape.98 = bf16[96,4096]{1,0:T(8,128)(2,1)} reshape(bf16[8,12,4096]{2,1,0:T(8,128)(2,1)} %all_to_all.29) | data formatting | bytes 1572864 | tf_op jit(solution)/shard_map/reshape | solution.py:50
  130.3 2.9 %fusion.4 = f32[96,384]{1,0:T(8,128)S(1)} fusion(bf16[96,4096]{1,0:T(8,128)(2,1)} %reshape.98, bf16[1,4096,384]{2,1,0:T(8,128)(2,1)} %param.25), kind=kOutput, calls=%fused_computation.5 | convolution fusion | flops 301989888 | bytes 4079616 | tf_op jit(solution)/shard_map/dot_general | solution.py:51
  133.6 1.3 fusion.11
  134.9 0.9 dot_general.40
  135.8 2.0 fusion
  137.8 4.5 %all-to-all-start.2 = ((f32[8,12,4096]{2,1,0:T(8,128)}), f32[8,12,4096]{2,1,0:T(8,128)}, u32[]{:S(2)}, u32[]{:S(2)}) async-start(f32[8,12,4096]{2,1,0:T(8,128)} %fusion), calls=%async_computation.2 | async-start | bytes 4194304 | tf_op jit(solution)/shard_map/all_to_all | solution.py:116
  142.7 47.4 %all-to-all-done.2 = f32[8,12,4096]{2,1,0:T(8,128)} async-done(((f32[8,12,4096]{2,1,0:T(8,128)}), f32[8,12,4096]{2,1,0:T(8,128)}, u32[]{:S(2)}, u32[]{:S(2)}) %all-to-all-start.2) | async-done | bytes 1572896 | tf_op jit(solution)/shard_map/all_to_all | solution.py:116
  190.1 2.7 %reshape.99 = f32[2,48,4096]{2,1,0:T(8,128)} reshape(f32[8,12,4096]{2,1,0:T(8,128)} %all-to-all-done.2) | data formatting | bytes 3145728 | tf_op jit(solution)/shard_map/reshape | solution.py:117
  192.8 2.5 %reduce_sum.72 = f32[48,4096]{1,0:T(8,128)} reduce(f32[2,48,4096]{2,1,0:T(8,128)} %reshape.99, f32[]{:T(128)} %constant.16.clone.1), dimensions={0}, to_apply=%region_10.11 | reduce | flops 196608 | bytes 2359300 | tf_op jit(solution)/shard_map/reduce_sum | solution.py:117
  195.3 2.3 %fusion.32 = f32[16,4096]{1,0:T(8,128)} fusion(f32[16,48]{1,0:T(8,128)S(1)} %select_reduce_fusion, f32[48,4096]{1,0:T(8,128)} %reduce_sum.72), kind=kOutput, calls=%fused_computation.53 | convolution fusion | flops 37748736 | bytes 1051648 | tf_op jit(solution)/shard_map/dot_general | solution.py:118
  197.6 6.8 %reduce-scatter.2.cloned.1.call-done = f32[16,2048]{1,0:T(8,128)} async-done(((f32[16,4096]{1,0:T(8,128)}), f32[16,2048]{1,0:T(8,128)}) %reduce-scatter.2.cloned.1.call-update) | async-done | bytes 131088 | tf_op jit(solution)/shard_map/reduce_scatter | solution.py:124
  204.4 1.5 add_convert_fusion
  (44 shorter events, 6.0 us)
Async XLA Ops:
  6.5 129.2 %copy-start = (bf16[1,384,4096]{2,1,0:T(8,128)(2,1)S(1)}, bf16[1,384,4096]{2,1,0:T(8,128)(2,1)}, u32[]{:S(2)}) copy-start(bf16[1,384,4096]{2,1,0:T(8,128)(2,1)} %param.27) | copy-start | bytes 9437188
  6.5 51.2 %all-gather.2.cloned.1.call-start = ((), (), s32[]{:S(2)}) async-start(), calls=%async_computation.4 | async-start | bytes 1179648 | tf_op jit(solution)/shard_map/all_gather | solution.py:83
  14.7 50.5 %copy-start.5 = (bf16[4096]{0:T(1024)(128)(2,1)S(1)}, bf16[4096]{0:T(1024)(128)(2,1)}, u32[]{:S(2)}) copy-start(bf16[4096]{0:T(1024)(128)(2,1)} %param.23) | copy-start | bytes 24580
  14.7 50.6 %copy-start.4 = (s32[16,2]{0,1:T(2,128)S(1)}, s32[16,2]{0,1:T(2,128)}, u32[]{:S(2)}) copy-start(s32[16,2]{0,1:T(2,128)} %param.21) | copy-start | bytes 388
  61.7 11.7 %all-to-all-start = ((f32[8,16,512]{2,1,0:T(8,128)}), f32[8,16,512]{2,1,0:T(8,128)S(1)}, u32[]{:S(2)}, u32[]{:S(2)}) async-start(f32[8,16,512]{2,1,0:T(8,128)} %bitcast.58), calls=%async_computation | async-start | bytes 524288 | tf_op jit(solution)/shard_map/all_to_all | solution.py:85
  65.2 26.2 %all-reduce.2.cloned.1.call-start = ((), (), s32[]{:S(2)}) async-start(), calls=%async_computation.5 | async-start | bytes 524288 | tf_op jit(solution)/shard_map/psum | solution.py:87
  130.3 2.9 %copy-start.1 = (bf16[96,4096]{1,0:T(8,128)(2,1)S(1)}, bf16[96,4096]{1,0:T(8,128)(2,1)}, u32[]{:S(2)}) copy-start(bf16[96,4096]{1,0:T(8,128)(2,1)} %reshape.98) | copy-start | bytes 2359300
  130.3 3.3 %copy-start.2 = (bf16[1,4096,384]{2,1,0:T(8,128)(2,1)S(1)}, bf16[1,4096,384]{2,1,0:T(8,128)(2,1)}, u32[]{:S(2)}) copy-start(bf16[1,4096,384]{2,1,0:T(8,128)(2,1)} %param.26) | copy-start | bytes 9437188
  137.8 4.5 %copy-start.3 = (bf16[4096,4]{0,1:T(4,128)(2,1)S(1)}, bf16[4096,4]{0,1:T(4,128)(2,1)}, u32[]{:S(2)}) copy-start(bf16[4096,4]{0,1:T(4,128)(2,1)} %param.24) | copy-start | bytes 98308
  137.8 52.3 %all-to-all-start.2 = ((f32[8,12,4096]{2,1,0:T(8,128)}), f32[8,12,4096]{2,1,0:T(8,128)}, u32[]{:S(2)}, u32[]{:S(2)}) async-start(f32[8,12,4096]{2,1,0:T(8,128)} %fusion), calls=%async_computation.2 | async-start | bytes 4194304 | tf_op jit(solution)/shard_map/all_to_all | solution.py:116
  142.3 62.2 %reduce-scatter.2.cloned.1.call-start = ((), (), s32[]{:S(2)}) async-start(), calls=%async_computation.6 | async-start | bytes 393216 | tf_op jit(solution)/shard_map/reduce_scatter | solution.py:124
Sparse Core Ops, SparseCore 0:
  14.8 42.9 all-gather.1
  74.3 17.0 all-reduce.1
  197.8 6.6 reduce-scatter.1
where the time goes:
time: 213 us
  waiting for transfers between devices  122 us (57%)
  blocking collectives  32.1 us (15%)
  matrix products  16.9 us (8%)
  between operations  13.3 us (6%)
  local copies, waits for them, and re-layouts  12.6 us (6%)
  starting transfers between devices  7.97 us (4%)
  other arithmetic  7.74 us (4%)
    all_to_all x1, waiting for transfers between devices, shards(): lax.all_to_all(result, 'dev', split_axis=0, concat_axis=0, tiled=True)  47.4 us
    all_gather x1, waiting for transfers between devices, shards(): lax.all_gather(attn, 'dev', axis=0, tiled=True)  43.1 us
    all_to_all x1, blocking collectives, shards(): lax.all_to_all(outgoing, 'dev', split_axis=0, concat_axis=0, tiled=True)  32.1 us
    psum x1, waiting for transfers between devices, shards(): h_one = lax.psum(partial_home, 'tp') + residual  17.1 us
    all_to_all x1, waiting for transfers between devices, shards(): lax.all_to_all(projected, 'dev', split_axis=0, concat_axis=1, tiled=True)  7.53 us
    reduce_scatter x1, waiting for transfers between devices, shards(): moe = lax.psum_scatter(moe, 'tp', scatter_dimension=1, tiled=True)  6.81 us
    all_to_all x1, starting transfers between devices, shards(): lax.all_to_all(result, 'dev', split_axis=0, concat_axis=0, tiled=True)  4.47 us
  transfers between devices with their start and end apart: 5, of which 5 were waited for; matrix products, arithmetic and copies ran while one was open for 1% of the time, Pallas kernels for 0%

commit v1 on v0

v1 whole, which is shorter than its diff:
```python
import functools
import math

import jax
import jax.numpy as jnp
from jax import lax
from jax.experimental import pallas as pl
from jax.experimental.pallas import tpu as pltpu
from jax.sharding import PartitionSpec as P

HEAD = 128
EPS = 1e-06
F32 = jnp.float32
BF16 = jnp.bfloat16
NT = (((1,), (1,)), ((), ()))


def layer_kernel(
    n, experts,
    len_ref, h_ref, q_ref, fk_ref, fv_ref, routes_ref, gain_ref, rw_ref,
    kc_hbm, vc_hbm, wo_hbm, wg_hbm, wu_hbm, wd_hbm,
    out_ref,
    kc, vc, wo, wg, wu, wd,
    qs, fkf, fvf, sc, pn, pw, ob,
    ag, pacc, pbuf, pr, h1, xg, act, ysib, yin, yacc, sbuf, rbuf,
    lsem, ag_s, ag_r, af_s, af_r, p_s, p_r, ps_s, ps_r,
    x_s, x_r, xf_s, xf_r, xs_s, xs_r, y_s, y_r, m_s, m_r,
):
    d = lax.axis_index("dev")
    c = lax.axis_index("tp")
    tp = 2
    cols = n // 2
    a = d // 2
    b = d % 2
    twin = a * 2 + (1 - b)
    rows = q_ref.shape[0]
    width = h_ref.shape[1]
    half = width // tp
    kvh = fk_ref.shape[1] // HEAD
    heads = q_ref.shape[1] // HEAD
    per = heads // kvh
    kpart = per * HEAD
    cw = wo.shape[1]
    ep = rw_ref.shape[0] // 2

    local = [
        pltpu.make_async_copy(src, dst, lsem.at[i])
        for i, (src, dst) in enumerate(
            [(kc_hbm, kc), (vc_hbm, vc), (wo_hbm, wo), (wg_hbm.at[0], wg), (wu_hbm.at[0], wu), (wd_hbm.at[0], wd)]
        )
    ]
    for cp in local:
        cp.start()

    barrier = pltpu.get_barrier_semaphore()
    for k in range(1, n):
        pl.semaphore_signal(
            barrier, inc=1, device_id={"dev": lax.rem(d + k, n)}, device_id_type=pl.DeviceIdType.MESH
        )
    pl.semaphore_signal(barrier, inc=1, device_id={"tp": 1 - c}, device_id_type=pl.DeviceIdType.MESH)

    def send(src, dst, ssem, rsem, **to):
        cp = pltpu.make_async_remote_copy(
            src_ref=src, dst_ref=dst, send_sem=ssem, recv_sem=rsem,
            device_id=to, device_id_type=pl.DeviceIdType.MESH,
        )
        cp.start()
        return cp

    pending = []

    for hh in range(heads):
        qs[pl.ds(hh, rows, stride=heads), :] = q_ref[:, hh * HEAD:(hh + 1) * HEAD].astype(F32)
    for g in range(kvh):
        fkf[g] = fk_ref[:, g * HEAD:(g + 1) * HEAD].astype(F32)
        fvf[g] = fv_ref[:, g * HEAD:(g + 1) * HEAD].astype(F32)
    factor = 1.0 / math.sqrt(HEAD)
    local[0].wait()
    slots = kc.shape[1]
    lane = lax.broadcasted_iota(jnp.int32, (per, slots), 1)
    step = 4

    @pl.loop(0, rows, step=step)
    def _(r0):
        for i in range(step):
            r = r0 + i
            live = lane < len_ref[r]
            for g in range(kvh):
                at = pl.ds(pl.multiple_of(r * heads + g * per, per), per)
                q = qs[at, :]
                s = lax.dot_general(
                    q.astype(BF16), kc[r, :, g * HEAD:(g + 1) * HEAD], NT, preferred_element_type=F32
                )
                sc[at, :] = jnp.where(live, s * factor, -1e30)
                pn[at, :] = q * fkf[g, pl.ds(r, 1), :]

    chunk = 128

    @pl.loop(0, rows * heads, step=chunk)
    def _(r0):
        at = pl.ds(pl.multiple_of(r0, chunk), chunk)
        s = sc[at, :]
        sn = jnp.sum(pn[at, :], -1, keepdims=True) * factor
        m = jnp.maximum(jnp.max(s, -1, keepdims=True), sn)
        p = jnp.exp(s - m)
        en = jnp.exp(sn - m)
        tot = jnp.sum(p, -1, keepdims=True) + en
        pw[at, :] = (p / tot).astype(BF16)
        pn[at, :] = jnp.broadcast_to((en / tot).astype(BF16).astype(F32), (chunk, HEAD))

    local[1].wait()

    @pl.loop(0, rows, step=step)
    def _(r0):
        for i in range(step):
            r = r0 + i
            for g in range(kvh):
                at = pl.ds(pl.multiple_of(r * heads + g * per, per), per)
                o = jnp.dot(pw[at, :], vc[r, :, g * HEAD:(g + 1) * HEAD], preferred_element_type=F32)
                ob[at, :] = o + pn[at, :] * fvf[g, pl.ds(r, 1), :]

    pl.semaphore_wait(barrier, n)

    sent = []
    for g in range(kvh):
        for hh in range(per):
            ag[g, d, :, hh * HEAD:(hh + 1) * HEAD] = ob[
                pl.ds(g * per + hh, rows, stride=heads), :
            ].astype(BF16)
        blk = ag.at[g, d]
        one = [send(blk, blk, af_s.at[g, 0], af_r.at[g, 0], dev=twin)]
        for k in range(1, cols):
            j = lax.rem(a + k, cols) * 2 + b
            one.append(send(blk, blk, ag_s.at[g, k], ag_r.at[g, k], dev=j))
        sent.append(one)
    fwd = []
    for g in range(kvh):
        for k in range(1, cols):
            sent[g][k].wait_recv()
            src = lax.rem(a + cols - k, cols) * 2 + b
            blk = ag.at[g, src]
            fwd.append(send(blk, blk, af_s.at[g, k], af_r.at[g, k], dev=twin))
    local[2].wait()
    blocks = min(n, 128 // rows)
    mrows = blocks * rows
    for g in range(kvh):
        sent[g][0].wait_recv()
        for k in range(1, cols):
            fwd[g * (cols - 1) + k - 1].wait_recv()

        @pl.loop(0, n, step=blocks)
        def _(j0):
            x = ag[g, pl.ds(j0, blocks)].reshape(mrows, kpart)
            y = jnp.dot(x, wo[g * kpart:(g + 1) * kpart, :], preferred_element_type=F32)
            y = y.reshape(blocks, rows, cw)
            if g == 0:
                pacc[pl.ds(j0, blocks)] = y
            else:
                y = y + pacc[pl.ds(j0, blocks)]
                pacc[pl.ds(j0, blocks)] = y
            if g == kvh - 1:
                pbuf[pl.ds(j0, blocks)] = y.astype(BF16)
    for one in sent:
        pending += one
    pending += fwd

    hops = []
    for k in range(1, n):
        j = lax.rem(d + k, n)
        hops.append(send(pbuf.at[j], pr.at[c, d], p_s.at[k], p_r.at[k], dev=j))
    pr[c, d] = pbuf[d]
    sib = [send(pr.at[c, d], pr.at[c, d], ps_s.at[0], ps_r.at[0], tp=1 - c)]
    for k in range(1, n):
        hops[k - 1].wait_recv()
        src = lax.rem(d + n - k, n)
        sib.append(send(pr.at[c, src], pr.at[c, src], ps_s.at[k], ps_r.at[k], tp=1 - c))
    for cp in sib:
        cp.wait_recv()
    pending += hops + sib

    ss = jnp.zeros((rows, 1), F32)
    for j in range(n):
        at = slice(j * cw, (j + 1) * cw)
        v = h_ref[:, at].astype(F32) + (pr[0, j].astype(F32) + pr[1, j].astype(F32))
        h1[:, at] = v
        ss = ss + jnp.sum(v * v, -1, keepdims=True)
    scale = lax.rsqrt(ss / width + EPS)
    logits = jnp.zeros((rows, 2 * ep), F32)
    for t in range(tp):
        at = slice(t * half, (t + 1) * half)
        x2 = (h1[:, at] * scale * gain_ref[:, at].astype(F32)).astype(BF16)
        xg[t, d, :, 0:half] = x2
        logits = logits + lax.dot_general(x2, rw_ref[:, at], NT, preferred_element_type=F32)
    spot = lax.broadcasted_iota(jnp.int32, (rows, 2 * ep), 1)
    expert = jnp.where(spot >= ep, spot - ep, spot)
    chosen = jnp.zeros((rows, 2 * ep), jnp.bool_)
    for k in range(routes_ref.shape[1]):
        chosen = chosen | (expert == routes_ref[:, k:k + 1])
    expo = jnp.where(chosen, jnp.exp(logits), 0.0)
    gates = expo / jnp.sum(jnp.where(spot < ep, expo, 0.0), -1, keepdims=True)
    high = gates.astype(BF16).astype(F32)
    ext = jnp.where(spot < ep, high, gates - high).astype(BF16)
    for t in range(tp):
        xg[t, d, :, half:half + HEAD] = jnp.zeros((rows, HEAD), BF16)
        xg[t, d, :, half:half + 2 * ep] = ext

    blk = xg.at[c, d]
    first = [send(blk, blk, xf_s.at[0], xf_r.at[0], dev=twin)]
    for k in range(1, cols):
        j = lax.rem(a + k, cols) * 2 + b
        first.append(send(blk, blk, x_s.at[k], x_r.at[k], dev=j))
    sib = []
    xfw = []
    for k in range(1, cols):
        first[k].wait_recv()
        src = lax.rem(a + cols - k, cols) * 2 + b
        blk = xg.at[c, src]
        xfw.append(send(blk, blk, xf_s.at[k], xf_r.at[k], dev=twin))
        sib.append(send(blk, blk, xs_s.at[k], xs_r.at[k], tp=1 - c))
    for k in range(cols):
        (first[0] if k == 0 else xfw[k - 1]).wait_recv()
        src = lax.rem(a + cols - k, cols) * 2 + (1 - b)
        blk = xg.at[c, src]
        sib.append(send(blk, blk, xs_s.at[cols + k], xs_r.at[cols + k], tp=1 - c))
    for cp in sib:
        cp.wait_recv()
    pending += first + xfw + sib

    local[3].wait()
    local[4].wait()
    local[5].wait()
    mine = lax.rem(d, experts)
    other = pl.multiple_of((1 - c) * half, half)
    own = pl.multiple_of(c * half, half)

    @pl.loop(0, n, step=blocks)
    def _(j0):
        x0 = xg[0, pl.ds(j0, blocks), :, 0:half].reshape(mrows, half)
        x1 = xg[1, pl.ds(j0, blocks), :, 0:half].reshape(mrows, half)
        gt = jnp.dot(x0, wg[0:half, :], preferred_element_type=F32)
        gt = gt + jnp.dot(x1, wg[half:, :], preferred_element_type=F32)
        up = jnp.dot(x0, wu[0:half, :], preferred_element_type=F32)
        up = up + jnp.dot(x1, wu[half:, :], preferred_element_type=F32)
        act[pl.ds(j0, blocks)] = (
            (gt / (1.0 + jnp.exp(-gt)) * up).astype(BF16).reshape(blocks, rows, act.shape[2])
        )

    def weight_of(j0):
        e = xg[0, pl.ds(j0, blocks), :, half:half + HEAD].reshape(mrows, HEAD).astype(F32)
        ln = lax.broadcasted_iota(jnp.int32, (mrows, HEAD), 1)
        return jnp.sum(jnp.where((ln == mine) | (ln == mine + ep), e, 0.0), -1, keepdims=True)

    @pl.loop(0, n, step=blocks)
    def _(j0):
        w = weight_of(j0)
        x = act[pl.ds(j0, blocks)].reshape(mrows, act.shape[2])
        y = jnp.dot(x, wd[:, pl.ds(other, half)], preferred_element_type=F32) * w
        ysib[pl.ds(j0, blocks)] = y.astype(BF16).reshape(blocks, rows, half)

    ycp = send(ysib, yin, y_s, y_r, tp=1 - c)

    @pl.loop(0, n, step=blocks)
    def _(j0):
        w = weight_of(j0)
        x = act[pl.ds(j0, blocks)].reshape(mrows, act.shape[2])
        y = jnp.dot(x, wd[:, pl.ds(own, half)], preferred_element_type=F32) * w
        yacc[pl.ds(j0, blocks)] = y.reshape(blocks, rows, half)

    ycp.wait_recv()
    hops = []
    for k in range(1, n):
        j = lax.rem(d + k, n)
        sbuf[j] = (yacc[j] + yin[j].astype(F32)).astype(BF16)
        hops.append(send(sbuf.at[j], rbuf.at[k], m_s.at[k], m_r.at[k], dev=j))
    total = h1[:, pl.ds(own, half)] + (yacc[d] + yin[d].astype(F32))
    for k in range(1, n):
        hops[k - 1].wait_recv()
        total = total + rbuf[k].astype(F32)
    out_ref[...] = total.astype(BF16)
    pending += [ycp] + hops
    for cp in pending:
        cp.wait_send()


def shards(
    n, h_in, query, key_cache, cached_value_rows, fresh_token_key, fresh_token_value,
    lengths, routes, w_out, gain, router_weight, w_gate, w_up, w_down,
):
    rows, width = h_in.shape
    experts = router_weight.shape[1]
    ep = -(-experts // 16) * 16
    rw = jnp.pad(router_weight.T, ((0, ep - experts), (0, 0)))
    rw = jnp.concatenate([rw, rw], 0)
    half = width // 2
    kvh = fresh_token_key.shape[1] // HEAD
    heads = query.shape[1] // HEAD
    per = heads // kvh
    cw = w_out.shape[1]
    ff = w_gate.shape[2]
    cols = n // 2
    slots = key_cache.shape[1]
    vm = pl.BlockSpec(memory_space=pltpu.VMEM)
    anyw = pl.BlockSpec(memory_space=pl.ANY)
    dma = pltpu.SemaphoreType.DMA
    return pl.pallas_call(
        functools.partial(layer_kernel, n, experts),
        out_shape=jax.ShapeDtypeStruct((rows, half), BF16),
        in_specs=[pl.BlockSpec(memory_space=pltpu.SMEM)] + [vm] * 7 + [anyw] * 6,
        out_specs=vm,
        scratch_shapes=[
            pltpu.VMEM(key_cache.shape, BF16),
            pltpu.VMEM(cached_value_rows.shape, BF16),
            pltpu.VMEM(w_out.shape, BF16),
            pltpu.VMEM(w_gate.shape[1:], BF16),
            pltpu.VMEM(w_up.shape[1:], BF16),
            pltpu.VMEM(w_down.shape[1:], BF16),
            pltpu.VMEM((rows * heads, HEAD), F32),
            pltpu.VMEM((kvh, rows, HEAD), F32),
            pltpu.VMEM((kvh, rows, HEAD), F32),
            pltpu.VMEM((rows * heads, slots), F32),
            pltpu.VMEM((rows * heads, HEAD), F32),
            pltpu.VMEM((rows * heads, slots), BF16),
            pltpu.VMEM((rows * heads, HEAD), F32),
            pltpu.VMEM((kvh, n, rows, per * HEAD), BF16),
            pltpu.VMEM((n, rows, cw), F32),
            pltpu.VMEM((n, rows, cw), BF16),
            pltpu.VMEM((2, n, rows, cw), BF16),
            pltpu.VMEM((rows, width), F32),
            pltpu.VMEM((2, n, rows, half + HEAD), BF16),
            pltpu.VMEM((n, rows, ff), BF16),
            pltpu.VMEM((n, rows, half), BF16),
            pltpu.VMEM((n, rows, half), BF16),
            pltpu.VMEM((n, rows, half), F32),
            pltpu.VMEM((n, rows, half), BF16),
            pltpu.VMEM((n, rows, half), BF16),
            dma((6,)),
            dma((kvh, cols)), dma((kvh, cols)), dma((kvh, cols)), dma((kvh, cols)),
            dma((n,)), dma((n,)), dma((n,)), dma((n,)),
            dma((cols,)), dma((cols,)), dma((cols,)), dma((cols,)), dma((n,)), dma((n,)),
            dma, dma, dma((n,)), dma((n,)),
        ],
        compiler_params=pltpu.CompilerParams(
            collective_id=0, has_side_effects=True, vmem_limit_bytes=60 * 1024 * 1024
        ),
    )(
        lengths, h_in, query, fresh_token_key, fresh_token_value, routes, gain[None, :], rw,
        key_cache, cached_value_rows, w_out, w_gate, w_up, w_down,
    )


def solution(mesh):
    placed = (
        P(("groups", "dev"), None),
        P(("groups", "dev"), "tp"),
        P(("groups", "dev"), None, "tp"),
        P(("groups", "dev"), None, "tp"),
        P(("groups", "dev"), "tp"),
        P(("groups", "dev"), "tp"),
        P(("groups", "dev")),
        P(("groups", "dev"), None),
        P("tp", "dev"),
        P(),
        P(),
        P("dev", None, "tp"),
        P("dev", None, "tp"),
        P("dev", "tp", None),
    )
    return jax.shard_map(
        functools.partial(shards, mesh.shape["dev"]),
        mesh=mesh, in_specs=placed, out_specs=P(("groups", "dev"), "tp"), check_vma=False,
    )
```

time: 213 us -> 66.1 us (0.31)
  the two profiles are of different devices: /device:TPU:0 before, /device:TPU:14 now
where the time goes in v1:
time: 66.1 us; the launch traced here: 65.8 us
  Pallas kernels  60.2 us (91%)
  local copies, waits for them, and re-layouts  4.9 us (7%)
  other arithmetic  0.71 us (1%)
    pallas_call x1, Pallas kernels, shards(): pl.pallas_call(functools.partial(layer_kernel, n, experts), out_shape=jax...  60.2 us
    unnamed x2, local copies, waits for them, and re-layouts  2.82 us

profile of v1, /device:TPU:14, one launch (start us, length us, event | category | flops | bytes accessed | tf_op | source)
XLA Modules:
  0.0 65.8 jit_solution(6261317321515847707)
XLA Ops:
  0.0 0.8 %pad.4 = bf16[16,4096]{1,0:T(8,128)(2,1)S(1)} pad(bf16[4,4096]{1,0:T(4,128)(2,1)} %bitcast.1, bf16[]{:T(256)} %constant.2.clone.1), padding=0_12x0_0 | pad | bytes 163842 | tf_op jit(solution)/shard_map/jit(_pad)/pad | solution.py:292
  0.8 0.7 %pad_maximum_fusion.rw_ref = bf16[32,4096]{1,0:T(8,128)(2,1)} fusion(bf16[16,4096]{1,0:T(8,128)(2,1)S(1)} %pad.4), kind=kLoop, calls=%fused_computation | loop fusion | flops 524288 | bytes 393216 | tf_op jit(solution)/shard_map/concatenate | solution.py:293
  1.5 1.3 %broadcast_in_dim.3.gain_ref = bf16[1,4096]{1,0:T(2,128)(2,1)} reshape(bf16[4096]{0:T(1024)(128)(2,1)} %param.23) | data formatting | bytes 16384 | tf_op jit(solution)/shard_map/broadcast_in_dim | solution.py:346
  2.8 1.3 %copy.15.routes_ref = s32[16,2]{1,0:T(8,128)} copy(s32[16,2]{0,1:T(2,128)} %param.21) | data formatting | bytes 256 | tf_op args[7]
  4.1 60.2 %shard_map.136 = bf16[16,2048]{1,0:T(8,128)(2,1)} custom-call(s32[16]{0:T(128)} %len_ref.1, bf16[16,4096]{1,0:T(8,128)(2,1)} %h_ref.1, bf16[16,4096]{1,0:T(8,128)(2,1)} %q_ref.1, bf16[16,256]{1,0:T(8,128)(2,1)} %fk_ref.1, bf16[16,256]{1,0:T(8,128)(2,1)} %fv_ref.1, s32[16,2]{1,0:T(8,128)} %copy.15.routes_ref, bf16[1,4096]{1,0:T(2,128)(2,1)} %broadcast_in_dim.3.gain_ref, ...), custom_call_target="tpu_custom_call" | custom-call | tf_op jit(solution)/shard_map/pallas_call | solution.py:305
  64.3 1.5 %copy.17 = bf16[16,2048]{1,0:T(8,128)(2,1)} copy(bf16[16,2048]{1,0:T(8,128)(2,1)} %shard_map.136) | data formatting | bytes 131072

commit v2 on v1

v2 whole, which is shorter than its diff:
```python
import functools
import math

import jax
import jax.numpy as jnp
from jax import lax
from jax.experimental import pallas as pl
from jax.experimental.pallas import tpu as pltpu
from jax.sharding import PartitionSpec as P

HEAD = 128
EPS = 1e-06
F32 = jnp.float32
BF16 = jnp.bfloat16
NT = (((1,), (1,)), ((), ()))


def layer_kernel(
    n, experts,
    len_ref, routes_ref, h_ref, q_ref, fk_ref, fv_ref, gain_ref, rw_ref,
    kc_hbm, vc_hbm, wo_hbm, wg_hbm, wu_hbm, wd_hbm,
    out_ref,
    kc, vc, wo, wg, wu, wd, rw,
    qs, fkf, fvf, sc, pn, pw, ob,
    ag, pbuf, pr, h1, xg, act, ysib, yin, yacc, sbuf, rbuf,
    lsem, a_s, a_r, p_s, p_r, ps_s, ps_r, x_s, x_r, xs_s, xs_r, y_s, y_r, m_s, m_r,
):
    d = lax.axis_index("dev")
    c = lax.axis_index("tp")
    hops = n // 2
    rows = q_ref.shape[0]
    width = h_ref.shape[1]
    half = width // 2
    quart = half // 2
    kvh = fk_ref.shape[1] // HEAD
    heads = q_ref.shape[1] // HEAD
    per = heads // kvh
    kpart = per * HEAD
    cw = wo.shape[1]
    ep = rw.shape[0] // 2

    odd = lax.rem(d, 2)
    pos = (1 - odd) * lax.div(d, 2) + odd * (n - 1 - lax.div(d, 2))

    def at_pos(k):
        p = lax.rem(pos + (k % n), n)
        back = lax.div(p, hops)
        return (1 - back) * 2 * p + back * (2 * (n - 1 - p) + 1)

    ahead = (at_pos(1), at_pos(-1))

    def limit(way, part):
        return hops if way == part else hops - 1

    def origin(way, step):
        return at_pos(-step if way == 0 else step)

    local = [
        pltpu.make_async_copy(src, dst, lsem.at[i])
        for i, (src, dst) in enumerate(
            [(kc_hbm, kc), (vc_hbm, vc), (wo_hbm, wo), (wg_hbm.at[0], wg), (wu_hbm.at[0], wu), (wd_hbm.at[0], wd)]
        )
    ]
    local[0].start()
    local[1].start()

    barrier = pltpu.get_barrier_semaphore()
    for k in range(1, n):
        pl.semaphore_signal(
            barrier, inc=1, device_id={"dev": lax.rem(d + k, n)}, device_id_type=pl.DeviceIdType.MESH
        )
    pl.semaphore_signal(barrier, inc=1, device_id={"tp": 1 - c}, device_id_type=pl.DeviceIdType.MESH)

    def send(src, dst, ssem, rsem, **to):
        cp = pltpu.make_async_remote_copy(
            src_ref=src, dst_ref=dst, send_sem=ssem, recv_sem=rsem,
            device_id=to, device_id_type=pl.DeviceIdType.MESH,
        )
        cp.start()
        return cp

    pending = []

    for hh in range(heads):
        qs[pl.ds(hh, rows, stride=heads), :] = q_ref[:, hh * HEAD:(hh + 1) * HEAD].astype(F32)
    for g in range(kvh):
        fkf[g] = fk_ref[:, g * HEAD:(g + 1) * HEAD].astype(F32)
        fvf[g] = fv_ref[:, g * HEAD:(g + 1) * HEAD].astype(F32)
    rw[...] = jnp.zeros(rw.shape, BF16)
    rw[0:experts, :] = rw_ref[...]
    rw[ep:ep + experts, :] = rw_ref[...]
    factor = 1.0 / math.sqrt(HEAD)
    slots = kc.shape[1]
    lane = lax.broadcasted_iota(jnp.int32, (per, slots), 1)
    step = 4
    chunk = 128
    moves = {}
    for g in range(kvh):
        if g == 0:
            local[0].wait()
            local[2].start()

        @pl.loop(0, rows, step=step)
        def _(r0):
            for i in range(step):
                r = r0 + i
                live = lane < len_ref[r]
                q = qs[pl.ds(pl.multiple_of(r * heads + g * per, per), per), :]
                at = pl.ds(pl.multiple_of(r * per, per), per)
                s = lax.dot_general(
                    q.astype(BF16), kc[r, :, g * HEAD:(g + 1) * HEAD], NT, preferred_element_type=F32
                )
                sc[at, :] = jnp.where(live, s * factor, -1e30)
                pn[at, :] = q * fkf[g, pl.ds(r, 1), :]

        @pl.loop(0, rows * per, step=chunk)
        def _(r0):
            at = pl.ds(pl.multiple_of(r0, chunk), chunk)
            s = sc[at, :]
            sn = jnp.sum(pn[at, :], -1, keepdims=True) * factor
            m = jnp.maximum(jnp.max(s, -1, keepdims=True), sn)
            p = jnp.exp(s - m)
            en = jnp.exp(sn - m)
            tot = jnp.sum(p, -1, keepdims=True) + en
            pw[at, :] = (p / tot).astype(BF16)
            pn[at, :] = jnp.broadcast_to((en / tot).astype(BF16).astype(F32), (chunk, HEAD))

        if g == 0:
            local[1].wait()
            for i in (3, 4, 5):
                local[i].start()

        @pl.loop(0, rows, step=step)
        def _(r0):
            for i in range(step):
                r = r0 + i
                at = pl.ds(pl.multiple_of(r * per, per), per)
                o = jnp.dot(pw[at, :], vc[r, :, g * HEAD:(g + 1) * HEAD], preferred_element_type=F32)
                ob[at, :] = o + pn[at, :] * fvf[g, pl.ds(r, 1), :]

        for hh in range(per):
            ag[g, d, :, hh * HEAD:(hh + 1) * HEAD] = ob[pl.ds(hh, rows, stride=per), :].astype(BF16)
        if g == 0:
            pl.semaphore_wait(barrier, n)
        blk = ag.at[g, d]
        for way in range(2):
            moves[way, g, 1] = send(blk, blk, a_s.at[way, g, 1], a_r.at[way, g, 1], dev=ahead[way])

    for st in range(1, hops + 1):
        for g in range(kvh):
            for way in range(2):
                top = limit(way, g % 2)
                if st <= top:
                    moves[way, g, st].wait_recv()
                if st < top:
                    blk = ag.at[g, origin(way, st)]
                    moves[way, g, st + 1] = send(
                        blk, blk, a_s.at[way, g, st + 1], a_r.at[way, g, st + 1], dev=ahead[way]
                    )
    pending += list(moves.values())
    local[2].wait()
    blocks = min(n, 128 // rows)
    mrows = blocks * rows

    @pl.loop(0, n, step=blocks)
    def _(j0):
        y = jnp.zeros((mrows, cw), F32)
        for g in range(kvh):
            x = ag[g, pl.ds(j0, blocks)].reshape(mrows, kpart)
            y = y + jnp.dot(x, wo[g * kpart:(g + 1) * kpart, :], preferred_element_type=F32)
        pbuf[pl.ds(j0, blocks)] = y.astype(BF16).reshape(blocks, rows, cw)

    out = []
    for k in range(1, n):
        j = lax.rem(d + k, n)
        out.append(send(pbuf.at[j], pr.at[c, d], p_s.at[k], p_r.at[k], dev=j))
    pr[c, d] = pbuf[d]
    sib = [send(pr.at[c, d], pr.at[c, d], ps_s.at[0], ps_r.at[0], tp=1 - c)]
    for k in range(1, n):
        out[k - 1].wait_recv()
        src = lax.rem(d + n - k, n)
        sib.append(send(pr.at[c, src], pr.at[c, src], ps_s.at[k], ps_r.at[k], tp=1 - c))
    for cp in sib:
        cp.wait_recv()
    pending += out + sib

    ss = jnp.zeros((rows, 1), F32)
    for j in range(n):
        at = slice(j * cw, (j + 1) * cw)
        v = h_ref[:, at].astype(F32) + (pr[0, j].astype(F32) + pr[1, j].astype(F32))
        h1[:, at] = v
        ss = ss + jnp.sum(v * v, -1, keepdims=True)
    scale = lax.rsqrt(ss / width + EPS)
    gain = gain_ref[...].astype(F32)
    for i in range(width // HEAD):
        x2 = (h1[:, i * HEAD:(i + 1) * HEAD] * scale * gain[i:i + 1, :]).astype(BF16)
        part, lo = divmod(i * HEAD, quart)
        xg[part, d, :, lo:lo + HEAD] = x2
    logits = jnp.zeros((rows, 2 * ep), F32)
    for part in range(4):
        logits = logits + lax.dot_general(
            xg[part, d, :, 0:quart], rw[:, part * quart:(part + 1) * quart], NT, preferred_element_type=F32
        )
    spot = lax.broadcasted_iota(jnp.int32, (rows, 2 * ep), 1)
    line = lax.broadcasted_iota(jnp.int32, (rows, 2 * ep), 0)
    expert = jnp.where(spot >= ep, spot - ep, spot)
    chosen = jnp.zeros((rows, 2 * ep), jnp.bool_)
    for k in range(routes_ref.shape[0]):
        named = jnp.zeros((rows, 2 * ep), jnp.int32)
        for r in range(rows):
            named = jnp.where(line == r, routes_ref[k, r], named)
        chosen = chosen | (expert == named)
    expo = jnp.where(chosen, jnp.exp(logits), 0.0)
    gates = expo / jnp.sum(jnp.where(spot < ep, expo, 0.0), -1, keepdims=True)
    high = gates.astype(BF16).astype(F32)
    ext = jnp.where(spot < ep, high, gates - high).astype(BF16)
    for part in (0, 2):
        xg[part, d, :, quart:quart + HEAD] = jnp.zeros((rows, HEAD), BF16)
        xg[part, d, :, quart:quart + 2 * ep] = ext

    def piece(q, src):
        return xg.at[2 * c + q, src] if q == 0 else xg.at[2 * c + q, src, :, 0:quart]

    moves = {}
    sib = []
    for q in range(2):
        for way in range(2):
            blk = piece(q, d)
            moves[way, q, 1] = send(blk, blk, x_s.at[way, q, 1], x_r.at[way, q, 1], dev=ahead[way])
    for st in range(1, hops + 1):
        for q in range(2):
            for way in range(2):
                top = limit(way, q)
                if st > top:
                    continue
                moves[way, q, st].wait_recv()
                blk = piece(q, origin(way, st))
                if st < top:
                    moves[way, q, st + 1] = send(
                        blk, blk, x_s.at[way, q, st + 1], x_r.at[way, q, st + 1], dev=ahead[way]
                    )
                sib.append(send(blk, blk, xs_s.at[way, q, st], xs_r.at[way, q, st], tp=1 - c))
    for cp in sib:
        cp.wait_recv()
    pending += list(moves.values()) + sib

    local[3].wait()
    local[4].wait()
    local[5].wait()
    mine = lax.rem(d, experts)

    @pl.loop(0, n, step=blocks)
    def _(j0):
        gt = jnp.zeros((mrows, wg.shape[1]), F32)
        up = gt
        for part in range(4):
            x = xg[part, pl.ds(j0, blocks), :, 0:quart].reshape(mrows, quart)
            at = slice(part * quart, (part + 1) * quart)
            gt = gt + jnp.dot(x, wg[at, :], preferred_element_type=F32)
            up = up + jnp.dot(x, wu[at, :], preferred_element_type=F32)
        act[pl.ds(j0, blocks)] = (
            (gt / (1.0 + jnp.exp(-gt)) * up).astype(BF16).reshape(blocks, rows, act.shape[2])
        )

    def expert_out(j0, start):
        e = xg[0, pl.ds(j0, blocks), :, quart:quart + HEAD].reshape(mrows, HEAD).astype(F32)
        ln = lax.broadcasted_iota(jnp.int32, (mrows, HEAD), 1)
        w = jnp.sum(jnp.where((ln == mine) | (ln == mine + ep), e, 0.0), -1, keepdims=True)
        x = act[pl.ds(j0, blocks)].reshape(mrows, act.shape[2])
        at = pl.ds(pl.multiple_of(start, quart), quart)
        return (jnp.dot(x, wd[:, at], preferred_element_type=F32) * w).reshape(blocks, rows, quart)

    pair = []
    for q in range(2):
        @pl.loop(0, n, step=blocks)
        def _(j0):
            ysib[q, pl.ds(j0, blocks)] = expert_out(j0, (1 - c) * half + q * quart).astype(BF16)

        pair.append(send(ysib.at[q], yin.at[q], y_s.at[q], y_r.at[q], tp=1 - c))

    moves = {}

    def own_part(q, j):
        return yacc[q, j] + yin[q, j].astype(F32)

    def pass_on(way, q, st, value):
        sbuf[way, q, st] = value.astype(BF16)
        moves[way, q, st] = send(
            sbuf.at[way, q, st], rbuf.at[way, q, st], m_s.at[way, q, st], m_r.at[way, q, st], dev=ahead[way]
        )

    for q in range(2):
        @pl.loop(0, n, step=blocks)
        def _(j0):
            yacc[q, pl.ds(j0, blocks)] = expert_out(j0, c * half + q * quart)

        pair[q].wait_recv()
        for way in range(2):
            pass_on(way, q, 1, own_part(q, origin(1 - way, limit(way, q))))
    total = [
        h1[:, pl.ds(pl.multiple_of(c * half + q * quart, quart), quart)] + own_part(q, d) for q in range(2)
    ]
    for st in range(1, hops + 1):
        for q in range(2):
            for way in range(2):
                top = limit(way, q)
                if st > top:
                    continue
                moves[way, q, st].wait_recv()
                got = rbuf[way, q, st].astype(F32)
                if st == top:
                    total[q] = total[q] + got
                else:
                    pass_on(way, q, st + 1, got + own_part(q, origin(1 - way, top - st)))
    for q in range(2):
        out_ref[:, q * quart:(q + 1) * quart] = total[q].astype(BF16)
    pending += pair + list(moves.values())
    for cp in pending:
        cp.wait_send()


def shards(
    n, h_in, query, key_cache, cached_value_rows, fresh_token_key, fresh_token_value,
    lengths, routes, w_out, gain, router_weight, w_gate, w_up, w_down,
):
    rows, width = h_in.shape
    experts = router_weight.shape[1]
    ep = -(-experts // 16) * 16
    half = width // 2
    kvh = fresh_token_key.shape[1] // HEAD
    heads = query.shape[1] // HEAD
    per = heads // kvh
    cw = w_out.shape[1]
    ff = w_gate.shape[2]
    hops = n // 2
    quart = half // 2
    slots = key_cache.shape[1]
    vm = pl.BlockSpec(memory_space=pltpu.VMEM)
    anyw = pl.BlockSpec(memory_space=pl.ANY)
    dma = pltpu.SemaphoreType.DMA
    return pl.pallas_call(
        functools.partial(layer_kernel, n, experts),
        out_shape=jax.ShapeDtypeStruct((rows, half), BF16),
        in_specs=[pl.BlockSpec(memory_space=pltpu.SMEM)] * 2 + [vm] * 6 + [anyw] * 6,
        out_specs=vm,
        scratch_shapes=[
            pltpu.VMEM(key_cache.shape, BF16),
            pltpu.VMEM(cached_value_rows.shape, BF16),
            pltpu.VMEM(w_out.shape, BF16),
            pltpu.VMEM(w_gate.shape[1:], BF16),
            pltpu.VMEM(w_up.shape[1:], BF16),
            pltpu.VMEM(w_down.shape[1:], BF16),
            pltpu.VMEM((2 * ep, width), BF16),
            pltpu.VMEM((rows * heads, HEAD), F32),
            pltpu.VMEM((kvh, rows, HEAD), F32),
            pltpu.VMEM((kvh, rows, HEAD), F32),
            pltpu.VMEM((rows * per, slots), F32),
            pltpu.VMEM((rows * per, HEAD), F32),
            pltpu.VMEM((rows * per, slots), BF16),
            pltpu.VMEM((rows * per, HEAD), F32),
            pltpu.VMEM((kvh, n, rows, per * HEAD), BF16),
            pltpu.VMEM((n, rows, cw), BF16),
            pltpu.VMEM((2, n, rows, cw), BF16),
            pltpu.VMEM((rows, width), F32),
            pltpu.VMEM((4, n, rows, quart + HEAD), BF16),
            pltpu.VMEM((n, rows, ff), BF16),
            pltpu.VMEM((2, n, rows, quart), BF16),
            pltpu.VMEM((2, n, rows, quart), BF16),
            pltpu.VMEM((2, n, rows, quart), F32),
            pltpu.VMEM((2, 2, hops + 1, rows, quart), BF16),
            pltpu.VMEM((2, 2, hops + 1, rows, quart), BF16),
            dma((6,)),
            dma((2, kvh, hops + 1)), dma((2, kvh, hops + 1)),
            dma((n,)), dma((n,)), dma((n,)), dma((n,)),
            dma((2, 2, hops + 1)), dma((2, 2, hops + 1)), dma((2, 2, hops + 1)), dma((2, 2, hops + 1)),
            dma((2,)), dma((2,)), dma((2, 2, hops + 1)), dma((2, 2, hops + 1)),
        ],
        compiler_params=pltpu.CompilerParams(
            collective_id=0, has_side_effects=True, vmem_limit_bytes=60 * 1024 * 1024
        ),
    )(
        lengths, routes.T, h_in, query, fresh_token_key, fresh_token_value,
        gain.reshape(-1, HEAD), router_weight.T,
        key_cache, cached_value_rows, w_out, w_gate, w_up, w_down,
    )


def solution(mesh):
    placed = (
        P(("groups", "dev"), None),
        P(("groups", "dev"), "tp"),
        P(("groups", "dev"), None, "tp"),
        P(("groups", "dev"), None, "tp"),
        P(("groups", "dev"), "tp"),
        P(("groups", "dev"), "tp"),
        P(("groups", "dev")),
        P(("groups", "dev"), None),
        P("tp", "dev"),
        P(),
        P(),
        P("dev", None, "tp"),
        P("dev", None, "tp"),
        P("dev", "tp", None),
    )
    return jax.shard_map(
        functools.partial(shards, mesh.shape["dev"]),
        mesh=mesh, in_specs=placed, out_specs=P(("groups", "dev"), "tp"), check_vma=False,
    )
```

time: 66.1 us -> 64.6 us (0.977)
  the two profiles are of different devices: /device:TPU:14 before, /device:TPU:0 now
where the time goes in v2:
time: 64.6 us; the launch traced here: 64.4 us
  Pallas kernels  62.9 us (97%)
  local copies, waits for them, and re-layouts  1.47 us (2%)
    pallas_call x1, Pallas kernels, shards(): pl.pallas_call(functools.partial(layer_kernel, n, experts), out_shape=jax...  62.9 us
    unnamed x1, local copies, waits for them, and re-layouts  1.47 us

profile of v2, /device:TPU:0, one launch (start us, length us, event | category | flops | bytes accessed | tf_op | source)
XLA Modules:
  0.0 64.4 jit_solution(17233097438198566091)
XLA Ops:
  0.0 62.9 %shard_map.136 = bf16[16,2048]{1,0:T(8,128)(2,1)} custom-call(s32[16]{0:T(128)} %len_ref.1, s32[2,16]{1,0:T(2,128)} %bitcast.5, bf16[16,4096]{1,0:T(8,128)(2,1)} %h_ref.1, bf16[16,4096]{1,0:T(8,128)(2,1)} %q_ref.1, bf16[16,256]{1,0:T(8,128)(2,1)} %fk_ref.1, bf16[16,256]{1,0:T(8,128)(2,1)} %fv_ref.1, bf16[32,128]{1,0:T(8,128)(2,1)} %bitcast.4, ...), custom_call_target="tpu_custom_call" | custom-call | tf_op jit(solution)/shard_map/pallas_call | solution.py:341
  62.9 1.5 %copy.16 = bf16[16,2048]{1,0:T(8,128)(2,1)} copy(bf16[16,2048]{1,0:T(8,128)(2,1)} %shard_map.136) | data formatting | bytes 131072

commit v3 on v2

v3 whole, which is shorter than its diff:
```python
import functools
import math

import jax
import jax.numpy as jnp
from jax import lax
from jax.experimental import pallas as pl
from jax.experimental.pallas import tpu as pltpu
from jax.sharding import PartitionSpec as P

HEAD = 128
EPS = 1e-06
F32 = jnp.float32
BF16 = jnp.bfloat16
NT = (((1,), (1,)), ((), ()))


def layer_kernel(
    n, experts,
    len_ref, routes_ref, h_ref, q_ref, fk_ref, fv_ref, gain_ref, rw_ref,
    kc_hbm, vc_hbm, wo_hbm, wg_hbm, wu_hbm, wd_hbm,
    out_ref,
    kc, vc, wo, wg, wu, wd, rw,
    qs, fkf, fvf, sc, pn, pw, ob,
    eb, he, ag, pacc, pin, hg, h1, x2s, wrow, act, ysib, yin, yacc, tbuf, tin, sbuf, zin, din,
    lsem, e_s, e_r, a_s, a_r, af_s, af_r, pp_s, pp_r, hd_s, hd_r, hz_s, hz_r, hf_s, hf_r, hs_s, hs_r,
    y_s, y_r, t_s, t_r, z_s, z_r, m_s, m_r,
):
    d = lax.axis_index("dev")
    c = lax.axis_index("tp")
    hops = n // 2
    rows = q_ref.shape[0]
    width = h_ref.shape[1]
    half = width // 2
    quart = half // 2
    kvh = fk_ref.shape[1] // HEAD
    heads = q_ref.shape[1] // HEAD
    per = heads // kvh
    kpart = per * HEAD
    cw = wo.shape[1]
    ep = rw.shape[0]
    blocks = min(n, 128 // rows)
    mrows = blocks * rows

    cols = hops
    a = lax.div(d, 2)
    b = lax.rem(d, 2)
    twin = a * 2 + 1 - b

    def up(k, side=0):
        return lax.rem(a + k, cols) * 2 + (1 - b if side else b)

    def down(k, side=0):
        return lax.rem(a + cols - k, cols) * 2 + (1 - b if side else b)

    local = [
        pltpu.make_async_copy(src, dst, lsem.at[i])
        for i, (src, dst) in enumerate(
            [(kc_hbm, kc), (vc_hbm, vc), (wo_hbm, wo), (wg_hbm.at[0], wg), (wu_hbm.at[0], wu), (wd_hbm.at[0], wd)]
        )
    ]
    local[0].start()
    local[1].start()

    barrier = pltpu.get_barrier_semaphore()
    for k in range(1, n):
        pl.semaphore_signal(
            barrier, inc=1, device_id={"dev": lax.rem(d + k, n)}, device_id_type=pl.DeviceIdType.MESH
        )
    pl.semaphore_signal(barrier, inc=1, device_id={"tp": 1 - c}, device_id_type=pl.DeviceIdType.MESH)

    def send(src, dst, ssem, rsem, **to):
        cp = pltpu.make_async_remote_copy(
            src_ref=src, dst_ref=dst, send_sem=ssem, recv_sem=rsem,
            device_id=to, device_id_type=pl.DeviceIdType.MESH,
        )
        cp.start()
        return cp

    pending = []

    for hh in range(heads):
        qs[pl.ds(hh, rows, stride=heads), :] = q_ref[:, hh * HEAD:(hh + 1) * HEAD].astype(F32)
    for g in range(kvh):
        fkf[g] = fk_ref[:, g * HEAD:(g + 1) * HEAD].astype(F32)
        fvf[g] = fv_ref[:, g * HEAD:(g + 1) * HEAD].astype(F32)
    rw[...] = jnp.zeros(rw.shape, BF16)
    rw[0:experts, :] = rw_ref[...]
    spot = lax.broadcasted_iota(jnp.int32, (rows, HEAD), 1)
    line = lax.broadcasted_iota(jnp.int32, (rows, HEAD), 0)
    chosen = jnp.zeros((rows, HEAD), F32)
    for k in range(routes_ref.shape[0]):
        named = jnp.zeros((rows, HEAD), jnp.int32)
        for r in range(rows):
            named = jnp.where(line == r, routes_ref[k, r], named)
        chosen = jnp.where(spot == named, 1.0, chosen)
    for j in range(n):
        eb[j, :, 0:cw] = h_ref[:, j * cw:(j + 1) * cw]
        eb[j, :, cw:cw + HEAD] = chosen.astype(BF16)
    factor = 1.0 / math.sqrt(HEAD)
    slots = kc.shape[1]
    lane = lax.broadcasted_iota(jnp.int32, (per, slots), 1)
    step = 4
    cuts = 2
    chunk = 128
    early = []
    first = {}
    for g in range(kvh):
        if g == 0:
            local[0].wait()
            local[2].start()

        @pl.loop(0, rows, step=step)
        def _(r0):
            for i in range(step):
                r = r0 + i
                live = lane < len_ref[r]
                q = qs[pl.ds(pl.multiple_of(r * heads + g * per, per), per), :]
                at = pl.ds(pl.multiple_of(r * per, per), per)
                s = lax.dot_general(
                    q.astype(BF16), kc[r, :, g * HEAD:(g + 1) * HEAD], NT, preferred_element_type=F32
                )
                sc[at, :] = jnp.where(live, s * factor, -1e30)
                pn[at, :] = q * fkf[g, pl.ds(r, 1), :]

        if g == 0:
            pl.semaphore_wait(barrier, n)
            for k in range(1, n):
                j = lax.rem(d + k, n)
                early.append(send(eb.at[j], he.at[d], e_s.at[k], e_r.at[k], dev=j))
            he[d] = eb[d]

        @pl.loop(0, rows * per, step=chunk)
        def _(r0):
            at = pl.ds(pl.multiple_of(r0, chunk), chunk)
            s = sc[at, :]
            sn = jnp.sum(pn[at, :], -1, keepdims=True) * factor
            m = jnp.maximum(jnp.max(s, -1, keepdims=True), sn)
            p = jnp.exp(s - m)
            en = jnp.exp(sn - m)
            tot = jnp.sum(p, -1, keepdims=True) + en
            pw[at, :] = (p / tot).astype(BF16)
            pn[at, :] = jnp.broadcast_to((en / tot).astype(BF16).astype(F32), (chunk, HEAD))

        if g == 0:
            local[1].wait()
            for i in (3, 4, 5):
                local[i].start()

        @pl.loop(0, rows, step=step)
        def _(r0):
            for i in range(step):
                r = r0 + i
                at = pl.ds(pl.multiple_of(r * per, per), per)
                o = jnp.dot(pw[at, :], vc[r, :, g * HEAD:(g + 1) * HEAD], preferred_element_type=F32)
                ob[at, :] = o + pn[at, :] * fvf[g, pl.ds(r, 1), :]

        for u in range(cuts):
            w = g * cuts + u
            for hh in range(per // cuts):
                ag[w, d, :, hh * HEAD:(hh + 1) * HEAD] = ob[
                    pl.ds(u * (per // cuts) + hh, rows, stride=per), :
                ].astype(BF16)
            blk = ag.at[w, d]
            for k in range(1, cols):
                first[w, k] = send(blk, blk, a_s.at[w, k], a_r.at[w, k], dev=up(k))
            first[w, 0] = send(blk, blk, af_s.at[w, 0], af_r.at[w, 0], dev=twin)
    pending += early
    fwd = {}
    for w in range(kvh * cuts):
        for k in range(1, cols):
            first[w, k].wait_recv()
            blk = ag.at[w, down(k)]
            fwd[w, k] = send(blk, blk, af_s.at[w, k], af_r.at[w, k], dev=twin)
    for w in range(kvh * cuts):
        first[w, 0].wait_recv()
        for k in range(1, cols):
            fwd[w, k].wait_recv()
    pending += list(first.values()) + list(fwd.values())
    local[2].wait()
    kpart = kpart // cuts

    @pl.loop(0, n, step=blocks)
    def _(j0):
        y = jnp.zeros((mrows, cw), F32)
        for w in range(kvh * cuts):
            x = ag[w, pl.ds(j0, blocks)].reshape(mrows, kpart)
            y = y + jnp.dot(x, wo[w * kpart:(w + 1) * kpart, :], preferred_element_type=F32)
        pacc[pl.ds(j0, blocks)] = y.reshape(blocks, rows, cw)

    swap = send(pacc.at[pl.ds((1 - c) * hops, hops)], pin, pp_s, pp_r, tp=1 - c)
    for k in range(1, n):
        early[k - 1].wait_recv()
    swap.wait_recv()
    pending.append(swap)
    part = hops // 2

    def rows_of(core, q):
        return pl.ds(core * hops + q * part, part)

    for q in range(2):
        at = rows_of(c, q)
        hg[d, at] = (
            pacc[at] + pin[q * part:(q + 1) * part] + he[at, :, 0:cw].astype(F32)
        ).astype(BF16)
    one = hg.at[d, rows_of(c, 0)]
    two = hg.at[d, rows_of(c, 1)]
    zs = {}
    ds = {}
    for k in range(1, cols):
        zs[k] = send(one, one, hz_s.at[k], hz_r.at[k], dev=up(k))
    zs[0] = send(one, one, hf_s.at[0], hf_r.at[0], dev=twin)
    for k in range(1, n):
        ds[k] = send(two, two, hd_s.at[k], hd_r.at[k], dev=lax.rem(d + k, n))
    sib = [
        send(hg.at[d, rows_of(c, q)], hg.at[d, rows_of(c, q)], hs_s.at[q, 0], hs_r.at[q, 0], tp=1 - c)
        for q in range(2)
    ]

    def to_sibling(q, i, src):
        blk = hg.at[src, rows_of(c, q)]
        sib.append(send(blk, blk, hs_s.at[q, i], hs_r.at[q, i], tp=1 - c))

    hf = {}
    for k in range(1, cols):
        zs[k].wait_recv()
        blk = hg.at[down(k), rows_of(c, 0)]
        hf[k] = send(blk, blk, hf_s.at[k], hf_r.at[k], dev=twin)
        to_sibling(0, k, down(k))
    zs[0].wait_recv()
    to_sibling(0, cols, twin)
    for k in range(1, n):
        ds[k].wait_recv()
        to_sibling(1, k, lax.rem(d + n - k, n))
    for k in range(1, cols):
        hf[k].wait_recv()
        to_sibling(0, cols + k, down(k, 1))
    for cp in sib:
        cp.wait_recv()
    pending += list(zs.values()) + list(ds.values()) + list(hf.values()) + sib

    mine = lax.rem(d, experts)
    gain = gain_ref[...].astype(F32)
    lanes = cw // HEAD

    @pl.loop(0, n, step=blocks)
    def _(j0):
        ss = jnp.zeros((mrows, HEAD), F32)
        for t in range(n):
            for i in range(lanes):
                v = hg[t, pl.ds(j0, blocks), :, i * HEAD:(i + 1) * HEAD].reshape(mrows, HEAD).astype(F32)
                ss = ss + v * v
        scale = lax.rsqrt(jnp.sum(ss, -1, keepdims=True) / width + EPS)
        here = pl.ds(pl.multiple_of(j0 * rows, mrows), mrows)
        for t in range(n):
            for i in range(lanes):
                v = hg[t, pl.ds(j0, blocks), :, i * HEAD:(i + 1) * HEAD].reshape(mrows, HEAD).astype(F32)
                at = t * lanes + i
                x2s[here, at * HEAD:(at + 1) * HEAD] = (v * scale * gain[at:at + 1, :]).astype(BF16)
        logits = lax.dot_general(x2s[here, :], rw[...], NT, preferred_element_type=F32)
        named = he[pl.ds(j0, blocks), :, cw:cw + HEAD].reshape(mrows, HEAD)[:, 0:ep].astype(F32) > 0.5
        expo = jnp.where(named, jnp.exp(logits), 0.0)
        spot = lax.broadcasted_iota(jnp.int32, (mrows, ep), 1)
        top = jnp.sum(jnp.where(spot == mine, expo, 0.0), -1, keepdims=True)
        wrow[here, :] = jnp.broadcast_to(top / jnp.sum(expo, -1, keepdims=True), (mrows, HEAD))

    for i in range(hops):
        h1[:, i * cw:(i + 1) * cw] = hg[c * hops + i, d].astype(F32)

    local[3].wait()
    local[4].wait()
    local[5].wait()

    @pl.loop(0, n, step=blocks)
    def _(j0):
        x = x2s[pl.ds(pl.multiple_of(j0 * rows, mrows), mrows), :]
        gt = jnp.dot(x, wg[...], preferred_element_type=F32)
        up_ = jnp.dot(x, wu[...], preferred_element_type=F32)
        act[pl.ds(j0, blocks)] = (
            (gt / (1.0 + jnp.exp(-gt)) * up_).astype(BF16).reshape(blocks, rows, act.shape[2])
        )

    def expert_out(j0, start):
        w = wrow[pl.ds(pl.multiple_of(j0 * rows, mrows), mrows), 0:1]
        x = act[pl.ds(j0, blocks)].reshape(mrows, act.shape[2])
        at = pl.ds(pl.multiple_of(start, quart), quart)
        return (jnp.dot(x, wd[:, at], preferred_element_type=F32) * w).reshape(blocks, rows, quart)

    pair = []
    for q in range(2):
        @pl.loop(0, n, step=blocks)
        def _(j0):
            ysib[q, pl.ds(j0, blocks)] = expert_out(j0, (1 - c) * half + q * quart).astype(BF16)

        pair.append(send(ysib.at[q], yin.at[q], y_s.at[q], y_r.at[q], tp=1 - c))

    def own_part(q, j):
        return yacc[q, j] + yin[q, j].astype(F32)

    def compute(q):
        @pl.loop(0, n, step=blocks)
        def _(j0):
            yacc[q, pl.ds(j0, blocks)] = expert_out(j0, c * half + q * quart)

        pair[q].wait_recv()

    compute(0)
    ts = {}
    for k in range(cols - 1, -1, -1):
        tbuf[k] = own_part(0, up(k, 1)).astype(BF16)
        ts[k] = send(tbuf.at[k], tin.at[k], t_s.at[k], t_r.at[k], dev=twin)
    compute(1)
    ds = {}
    for k in range(1, n):
        j = lax.rem(d + k, n)
        sbuf[k] = own_part(1, j).astype(BF16)
        ds[k] = send(sbuf.at[k], din.at[k], m_s.at[k], m_r.at[k], dev=j)
    zs = {}
    for k in range(cols - 1, 0, -1):
        ts[k].wait_recv()
        tbuf[cols + k] = (own_part(0, up(k)) + tin[k].astype(F32)).astype(BF16)
        zs[k] = send(tbuf.at[cols + k], zin.at[k], z_s.at[k], z_r.at[k], dev=up(k))
    total = [h1[:, q * quart:(q + 1) * quart] + own_part(q, d) for q in range(2)]
    ts[0].wait_recv()
    total[0] = total[0] + tin[0].astype(F32)
    for k in range(1, n):
        ds[k].wait_recv()
        total[1] = total[1] + din[k].astype(F32)
    for k in range(cols - 1, 0, -1):
        zs[k].wait_recv()
        total[0] = total[0] + zin[k].astype(F32)
    for q in range(2):
        out_ref[:, q * quart:(q + 1) * quart] = total[q].astype(BF16)
    pending += pair + list(ts.values()) + list(ds.values()) + list(zs.values())
    for cp in pending:
        cp.wait_send()


def shards(
    n, h_in, query, key_cache, cached_value_rows, fresh_token_key, fresh_token_value,
    lengths, routes, w_out, gain, router_weight, w_gate, w_up, w_down,
):
    rows, width = h_in.shape
    experts = router_weight.shape[1]
    ep = -(-experts // 16) * 16
    half = width // 2
    kvh = fresh_token_key.shape[1] // HEAD
    heads = query.shape[1] // HEAD
    per = heads // kvh
    cw = w_out.shape[1]
    ff = w_gate.shape[2]
    hops = n // 2
    quart = half // 2
    slots = key_cache.shape[1]
    vm = pl.BlockSpec(memory_space=pltpu.VMEM)
    anyw = pl.BlockSpec(memory_space=pl.ANY)
    dma = pltpu.SemaphoreType.DMA
    return pl.pallas_call(
        functools.partial(layer_kernel, n, experts),
        out_shape=jax.ShapeDtypeStruct((rows, half), BF16),
        in_specs=[pl.BlockSpec(memory_space=pltpu.SMEM)] * 2 + [vm] * 6 + [anyw] * 6,
        out_specs=vm,
        scratch_shapes=[
            pltpu.VMEM(key_cache.shape, BF16),
            pltpu.VMEM(cached_value_rows.shape, BF16),
            pltpu.VMEM(w_out.shape, BF16),
            pltpu.VMEM(w_gate.shape[1:], BF16),
            pltpu.VMEM(w_up.shape[1:], BF16),
            pltpu.VMEM(w_down.shape[1:], BF16),
            pltpu.VMEM((-(-experts // 16) * 16, width), BF16),
            pltpu.VMEM((rows * heads, HEAD), F32),
            pltpu.VMEM((kvh, rows, HEAD), F32),
            pltpu.VMEM((kvh, rows, HEAD), F32),
            pltpu.VMEM((rows * per, slots), F32),
            pltpu.VMEM((rows * per, HEAD), F32),
            pltpu.VMEM((rows * per, slots), BF16),
            pltpu.VMEM((rows * per, HEAD), F32),
            pltpu.VMEM((n, rows, cw + HEAD), BF16),
            pltpu.VMEM((n, rows, cw + HEAD), BF16),
            pltpu.VMEM((2 * kvh, n, rows, per * HEAD // 2), BF16),
            pltpu.VMEM((n, rows, cw), F32),
            pltpu.VMEM((hops, rows, cw), F32),
            pltpu.VMEM((n, n, rows, cw), BF16),
            pltpu.VMEM((rows, half), F32),
            pltpu.VMEM((n * rows, width), BF16),
            pltpu.VMEM((n * rows, HEAD), F32),
            pltpu.VMEM((n, rows, ff), BF16),
            pltpu.VMEM((2, n, rows, quart), BF16),
            pltpu.VMEM((2, n, rows, quart), BF16),
            pltpu.VMEM((2, n, rows, quart), F32),
            pltpu.VMEM((2 * hops, rows, quart), BF16),
            pltpu.VMEM((hops, rows, quart), BF16),
            pltpu.VMEM((n, rows, quart), BF16),
            pltpu.VMEM((hops, rows, quart), BF16),
            pltpu.VMEM((n, rows, quart), BF16),
            dma((6,)), dma((n,)), dma((n,)),
            dma((2 * kvh, hops)), dma((2 * kvh, hops)), dma((2 * kvh, hops)), dma((2 * kvh, hops)),
            dma, dma, dma((n,)), dma((n,)), dma((hops,)), dma((hops,)), dma((hops,)), dma((hops,)),
            dma((2, n)), dma((2, n)),
            dma((2,)), dma((2,)), dma((hops,)), dma((hops,)), dma((hops,)), dma((hops,)), dma((n,)), dma((n,)),
        ],
        compiler_params=pltpu.CompilerParams(
            collective_id=0, has_side_effects=True, vmem_limit_bytes=60 * 1024 * 1024
        ),
    )(
        lengths, routes.T, h_in, query, fresh_token_key, fresh_token_value,
        gain.reshape(-1, HEAD), router_weight.T,
        key_cache, cached_value_rows, w_out, w_gate, w_up, w_down,
    )


def solution(mesh):
    placed = (
        P(("groups", "dev"), None),
        P(("groups", "dev"), "tp"),
        P(("groups", "dev"), None, "tp"),
        P(("groups", "dev"), None, "tp"),
        P(("groups", "dev"), "tp"),
        P(("groups", "dev"), "tp"),
        P(("groups", "dev")),
        P(("groups", "dev"), None),
        P("tp", "dev"),
        P(),
        P(),
        P("dev", None, "tp"),
        P("dev", None, "tp"),
        P("dev", "tp", None),
    )
    return jax.shard_map(
        functools.partial(shards, mesh.shape["dev"]),
        mesh=mesh, in_specs=placed, out_specs=P(("groups", "dev"), "tp"), check_vma=False,
    )
```

time: 64.6 us -> 57.5 us (0.89)
  Pallas kernels: 62.9 us -> 55.8 us
    pallas_call x1, Pallas kernels: 62.9 us -> 55.8 us  [shards(): pl.pallas_call(functools.partial(layer_kernel, n, experts), out_shape=jax...]
where the time goes in v3:
time: 57.5 us; the launch traced here: 57.3 us
  Pallas kernels  55.8 us (97%)
  local copies, waits for them, and re-layouts  1.47 us (3%)
    pallas_call x1, Pallas kernels, shards(): pl.pallas_call(functools.partial(layer_kernel, n, experts), out_shape=jax...  55.8 us
    unnamed x1, local copies, waits for them, and re-layouts  1.47 us

profile of v3, /device:TPU:0, one launch (start us, length us, event | category | flops | bytes accessed | tf_op | source)
XLA Modules:
  0.0 57.3 jit_solution(15814127642276306903)
XLA Ops:
  0.0 55.8 %shard_map.136 = bf16[16,2048]{1,0:T(8,128)(2,1)} custom-call(s32[16]{0:T(128)} %len_ref.1, s32[2,16]{1,0:T(2,128)} %bitcast.5, bf16[16,4096]{1,0:T(8,128)(2,1)} %h_ref.1, bf16[16,4096]{1,0:T(8,128)(2,1)} %q_ref.1, bf16[16,256]{1,0:T(8,128)(2,1)} %fk_ref.1, bf16[16,256]{1,0:T(8,128)(2,1)} %fv_ref.1, bf16[32,128]{1,0:T(8,128)(2,1)} %bitcast.4, ...), custom_call_target="tpu_custom_call" | custom-call | tf_op jit(solution)/shard_map/pallas_call | solution.py:358
  55.8 1.5 %copy.16 = bf16[16,2048]{1,0:T(8,128)(2,1)} copy(bf16[16,2048]{1,0:T(8,128)(2,1)} %shard_map.136) | data formatting | bytes 131072

commit v4 on v3

--- a/solution.py
+++ b/solution.py
@@ -23,7 +23,7 @@
     kc, vc, wo, wg, wu, wd, rw,
     qs, fkf, fvf, sc, pn, pw, ob,
     eb, he, ag, pacc, pin, hg, h1, x2s, wrow, act, ysib, yin, yacc, tbuf, tin, sbuf, zin, din,
-    lsem, e_s, e_r, a_s, a_r, af_s, af_r, pp_s, pp_r, hd_s, hd_r, hz_s, hz_r, hf_s, hf_r, hs_s, hs_r,
+    lsem, e_s, e_r, a_s, a_r, pp_s, pp_r, hd_s, hd_r, hz_s, hz_r, hf_s, hf_r, hs_s, hs_r,
     y_s, y_r, t_s, t_r, z_s, z_r, m_s, m_r,
 ):
     d = lax.axis_index("dev")
@@ -52,6 +52,18 @@
 
     def down(k, side=0):
         return lax.rem(a + cols - k, cols) * 2 + (1 - b if side else b)
+
+    pos = (1 - b) * a + b * (n - 1 - a)
+
+    def at_pos(k):
+        p = lax.rem(pos + (k % n), n)
+        back = lax.div(p, hops)
+        return (1 - back) * 2 * p + back * (2 * (n - 1 - p) + 1)
+
+    ahead = (at_pos(1), at_pos(-1))
+
+    def limit(way, w):
+        return hops if way == w % 2 else hops - 1
 
     local = [
         pltpu.make_async_copy(src, dst, lsem.at[i])
@@ -100,7 +112,7 @@
     factor = 1.0 / math.sqrt(HEAD)
     slots = kc.shape[1]
     lane = lax.broadcasted_iota(jnp.int32, (per, slots), 1)
-    step = 4
+    step = rows
     cuts = 2
     chunk = 128
     early = []
@@ -162,21 +174,21 @@
                     pl.ds(u * (per // cuts) + hh, rows, stride=per), :
                 ].astype(BF16)
             blk = ag.at[w, d]
-            for k in range(1, cols):
-                first[w, k] = send(blk, blk, a_s.at[w, k], a_r.at[w, k], dev=up(k))
-            first[w, 0] = send(blk, blk, af_s.at[w, 0], af_r.at[w, 0], dev=twin)
+            for way in range(2):
+                first[way, w, 1] = send(blk, blk, a_s.at[way, w, 1], a_r.at[way, w, 1], dev=ahead[way])
     pending += early
-    fwd = {}
-    for w in range(kvh * cuts):
-        for k in range(1, cols):
-            first[w, k].wait_recv()
-            blk = ag.at[w, down(k)]
-            fwd[w, k] = send(blk, blk, af_s.at[w, k], af_r.at[w, k], dev=twin)
-    for w in range(kvh * cuts):
-        first[w, 0].wait_recv()
-        for k in range(1, cols):
-            fwd[w, k].wait_recv()
-    pending += list(first.values()) + list(fwd.values())
+    for st in range(1, hops + 1):
+        for w in range(kvh * cuts):
+            for way in range(2):
+                last = limit(way, w)
+                if st <= last:
+                    first[way, w, st].wait_recv()
+                if st < last:
+                    blk = ag.at[w, at_pos(-st if way == 0 else st)]
+                    first[way, w, st + 1] = send(
+                        blk, blk, a_s.at[way, w, st + 1], a_r.at[way, w, st + 1], dev=ahead[way]
+                    )
+    pending += list(first.values())
     local[2].wait()
     kpart = kpart // cuts
 
@@ -394,7 +406,7 @@
             pltpu.VMEM((hops, rows, quart), BF16),
             pltpu.VMEM((n, rows, quart), BF16),
             dma((6,)), dma((n,)), dma((n,)),
-            dma((2 * kvh, hops)), dma((2 * kvh, hops)), dma((2 * kvh, hops)), dma((2 * kvh, hops)),
+            dma((2, 2 * kvh, hops + 1)), dma((2, 2 * kvh, hops + 1)),
             dma, dma, dma((n,)), dma((n,)), dma((hops,)), dma((hops,)), dma((hops,)), dma((hops,)),
             dma((2, n)), dma((2, n)),
             dma((2,)), dma((2,)), dma((hops,)), dma((hops,)), dma((hops,)), dma((hops,)), dma((n,)), dma((n,)),

time: 57.5 us -> 55.5 us (0.965)
  Pallas kernels: 55.8 us -> 53.8 us
    pallas_call x1, Pallas kernels: 55.8 us -> 53.8 us  [shards(): pl.pallas_call(functools.partial(layer_kernel, n, experts), out_shape=jax...]
where the time goes in v4:
time: 55.5 us; the launch traced here: 55.3 us
  Pallas kernels  53.8 us (97%)
  local copies, waits for them, and re-layouts  1.47 us (3%)
    pallas_call x1, Pallas kernels, shards(): pl.pallas_call(functools.partial(layer_kernel, n, experts), out_shape=jax...  53.8 us
    unnamed x1, local copies, waits for them, and re-layouts  1.47 us

profile of v4, /device:TPU:0, one launch (start us, length us, event | category | flops | bytes accessed | tf_op | source)
XLA Modules:
  0.0 55.3 jit_solution(12849487361000564480)
XLA Ops:
  0.0 53.8 %shard_map.136 = bf16[16,2048]{1,0:T(8,128)(2,1)} custom-call(s32[16]{0:T(128)} %len_ref.1, s32[2,16]{1,0:T(2,128)} %bitcast.5, bf16[16,4096]{1,0:T(8,128)(2,1)} %h_ref.1, bf16[16,4096]{1,0:T(8,128)(2,1)} %q_ref.1, bf16[16,256]{1,0:T(8,128)(2,1)} %fk_ref.1, bf16[16,256]{1,0:T(8,128)(2,1)} %fv_ref.1, bf16[32,128]{1,0:T(8,128)(2,1)} %bitcast.4, ...), custom_call_target="tpu_custom_call" | custom-call | tf_op jit(solution)/shard_map/pallas_call | solution.py:370
  53.8 1.5 %copy.16 = bf16[16,2048]{1,0:T(8,128)(2,1)} copy(bf16[16,2048]{1,0:T(8,128)(2,1)} %shard_map.136) | data formatting | bytes 131072
